TPU v7x, 32 devices: a whole 2x2x4 slice. The times are simulated.
32 devices in a mesh: groups: 2 (over y), tm: 16 (over z, x, core).
Axes of the slice: x: 2, y: 2, z: 4, core: 2. Of those that a mesh axis runs over, the one named last changes fastest.
Arguments:
- observations: float32 [512, 16, 256], P(('groups', 'tm')), parts along dimension 0, may hold values from -6 to 6
- start_mean: float32 [32, 512], P('groups'), parts along dimension 0, may hold values from -6 to 6
- transition: float32 [512, 512], replicated, may hold values from -0.01 to 1
- obs_map: float32 [512, 256], replicated, may hold values from -0.009765625 to 0.009765625
- kalman_gain: float32 [256, 512], replicated, may hold values from -0.01171875 to 0.01171875
- smoother_gain: float32 [512, 512], replicated, may hold values from -0.01 to 1
Outputs:
- filtered: float32 [512, 16, 512], P(('groups', 'tm')), parts along dimension 0
- smoothed: float32 [512, 16, 512], P(('groups', 'tm')), parts along dimension 0
There are 2 independent parts, one for each index of `groups`. A program takes and returns all parts, laid end to end along the dimension named above; an argument that names none is the same for every part. Nothing has to cross between parts.
All inputs are finite; a program needn't handle non-finite values.
Results may differ from a plain program's by a relative error of at most 0.0003.
Values sent between devices are 32-bit elements; how exact they have to be, the bound alone decides.
A program may use at most 64 MiB of HBM per device.

v0:
```python
import jax
import jax.numpy as jnp
from jax import lax
from jax.sharding import PartitionSpec as P


def passed_along(x, axis, by):
    count = lax.axis_size(axis)
    pairs = [(i, i + by) for i in range(count) if 0 <= i + by < count]
    return lax.ppermute(x, axis, pairs)


def product(first_op, second_op):
    return jnp.dot(
        first_op, second_op, precision=lax.Precision.HIGHEST, preferred_element_type=jnp.float32
    )


def power_of(matrix, exponent):
    result = None
    squared = matrix
    while exponent > 0:
        if exponent % 2 == 1:
            result = squared
        exponent = exponent // 2
        if exponent > 0:
            squared = product(squared, squared)
    return result


def per_device(observations, start_mean, transition, obs_map, kalman_gain, smoother_gain):
    steps_local = observations.shape[0]
    devices = lax.axis_size("tm")
    position = lax.axis_index("tm")
    zeros_state = jnp.zeros(start_mean.shape, jnp.float32)
    forward_map = transition - product(product(transition, obs_map), kalman_gain)
    forward_power = power_of(forward_map, steps_local)
    backward_power = power_of(smoother_gain, steps_local)

    def advance(carried, observed):
        predicted = product(carried, transition)
        updated = predicted + product(observed - product(predicted, obs_map), kalman_gain)
        return (updated, updated)

    opening = jnp.where(position == 0, start_mean, zeros_state)
    local_end, local_filtered = lax.scan(advance, opening, observations)

    def forward_hop(hop_index, chain_state):
        ending, incoming = chain_state
        received = passed_along(ending, "tm", 1)
        return lax.cond(
            position == hop_index,
            lambda: (product(received, forward_power) + local_end, received),
            lambda: (ending, incoming),
        )

    unused, entering = lax.fori_loop(1, devices, forward_hop, (local_end, zeros_state))

    def carry_forward(carried, unused_item):
        advanced = product(carried, forward_map)
        return (advanced, advanced)

    unused, forward_fix = lax.scan(carry_forward, entering, None, length=steps_local)
    filtered = local_filtered + forward_fix
    last_device = position == devices - 1
    top_carry = jnp.where(last_device, product(filtered[-1], transition), zeros_state)

    def retreat(carried, current):
        smoothed_now = current + product(carried - product(current, transition), smoother_gain)
        return (smoothed_now, smoothed_now)

    first_value, local_smoothed = lax.scan(retreat, top_carry, filtered, reverse=True)

    def backward_hop(hop_index, chain_state):
        ending, incoming = chain_state
        received = passed_along(ending, "tm", -1)
        return lax.cond(
            position == devices - 1 - hop_index,
            lambda: (product(received, backward_power) + first_value, received),
            lambda: (ending, incoming),
        )

    unused, leaving = lax.fori_loop(1, devices, backward_hop, (first_value, zeros_state))

    def carry_backward(carried, unused_item):
        advanced = product(carried, smoother_gain)
        return (advanced, advanced)

    unused, backward_fix = lax.scan(carry_backward, leaving, None, length=steps_local, reverse=True)
    smoothed = local_smoothed + backward_fix
    return (filtered, smoothed)


def solution(mesh):
    in_specs = (P(("groups", "tm"), None, None), P("groups", None), P(), P(), P(), P())
    out_specs = (P(("groups", "tm"), None, None), P(("groups", "tm"), None, None))
    return jax.shard_map(
        per_device, mesh=mesh, in_specs=in_specs, out_specs=out_specs, check_vma=False
    )
```

profile of v0, /device:TPU:7, one launch (start us, length us, event | category | flops | bytes accessed | tf_op | source)
XLA Modules:
  0.0 325.1 jit_solution(7161295298881646766)
XLA Ops:
  1.7 53.3 %while.86 = (s32[]{:T(128)}, f32[16,512]{1,0:T(8,128)S(1)}, f32[16,16,512]{2,1,0:T(8,128)S(1)}, f32[512,512]{1,0:T(8,128)}, f32[16,16,256]{2,1,0:T(8,128)}, /*in...) while((s32[]{:T(128)}, f32[16,512]{1,0:T(8,128)S(1)}, f32[16,16,512]{2,1,0:T(8,128)S(1)}, ...), condition=%wide.region_1.2_spmd, body=%wide.region_0.1_spmd.sunk | while | flops 100675584 | bytes 4440185 | solution.py:46
  65.9 91.1 %while.87 = (s32[]{:T(128)}, f32[16,512]{1,0:T(8,128)S(1)}, f32[16,512]{1,0:T(8,128)S(1)}, s32[]{:T(128)}, f32[512,512]{1,0:T(8,128)S(1)}, /*index=5*/f32[16,512]{1,0:T(8,128)S(1)}, s32[]{:T(128)}) while((s32[]{:T(128)}, f32[16,512]{1,0:T(8,128)S(1)}, f32[16,512]{1,0:T(8,128)S(1)}, s32[]{:T(128)}, f32[512,512]{1,0:T(8,128)S(1)}, ...), condition=%wide.region_5.6_spmd, body=%wide.region_2.5_spmd.sunk | while | flops 50339844 | bytes 1343683 | solution.py:57
  70.6 5.1 %collective-permute-start = (f32[16,512]{1,0:T(8,128)S(1)}, f32[16,512]{1,0:T(8,128)S(1)}, u32[]{:S(2)}, u32[]{:S(2)}) collective-permute-start(f32[16,512]{1,0:T(8,128)S(1)} %get-tuple-element.875), channel_id=1, source_target_pairs={{0,1},{1,2},{2,3},{3,4},{4,5},{5,6},{6,7},{7,8},{8,9},{9,10},{10,1... | collective-permute-start | bytes 98312 | tf_op jit(solution)/shard_map/while/body/eval_jaxpr/ppermute | solution.py:10
  76.7 5.1 %collective-permute-start = (f32[16,512]{1,0:T(8,128)S(1)}, f32[16,512]{1,0:T(8,128)S(1)}, u32[]{:S(2)}, u32[]{:S(2)}) collective-permute-start(f32[16,512]{1,0:T(8,128)S(1)} %get-tuple-element.875), channel_id=1, source_target_pairs={{0,1},{1,2},{2,3},{3,4},{4,5},{5,6},{6,7},{7,8},{8,9},{9,10},{10,1... | collective-permute-start | bytes 98312 | tf_op jit(solution)/shard_map/while/body/eval_jaxpr/ppermute | solution.py:10
  83.5 4.5 %collective-permute-start = (f32[16,512]{1,0:T(8,128)S(1)}, f32[16,512]{1,0:T(8,128)S(1)}, u32[]{:S(2)}, u32[]{:S(2)}) collective-permute-start(f32[16,512]{1,0:T(8,128)S(1)} %get-tuple-element.875), channel_id=1, source_target_pairs={{0,1},{1,2},{2,3},{3,4},{4,5},{5,6},{6,7},{7,8},{8,9},{9,10},{10,1... | collective-permute-start | bytes 98312 | tf_op jit(solution)/shard_map/while/body/eval_jaxpr/ppermute | solution.py:10
  89.0 5.8 %collective-permute-start = (f32[16,512]{1,0:T(8,128)S(1)}, f32[16,512]{1,0:T(8,128)S(1)}, u32[]{:S(2)}, u32[]{:S(2)}) collective-permute-start(f32[16,512]{1,0:T(8,128)S(1)} %get-tuple-element.875), channel_id=1, source_target_pairs={{0,1},{1,2},{2,3},{3,4},{4,5},{5,6},{6,7},{7,8},{8,9},{9,10},{10,1... | collective-permute-start | bytes 98312 | tf_op jit(solution)/shard_map/while/body/eval_jaxpr/ppermute | solution.py:10
  95.8 5.1 %collective-permute-start = (f32[16,512]{1,0:T(8,128)S(1)}, f32[16,512]{1,0:T(8,128)S(1)}, u32[]{:S(2)}, u32[]{:S(2)}) collective-permute-start(f32[16,512]{1,0:T(8,128)S(1)} %get-tuple-element.875), channel_id=1, source_target_pairs={{0,1},{1,2},{2,3},{3,4},{4,5},{5,6},{6,7},{7,8},{8,9},{9,10},{10,1... | collective-permute-start | bytes 98312 | tf_op jit(solution)/shard_map/while/body/eval_jaxpr/ppermute | solution.py:10
  101.9 5.1 %collective-permute-start = (f32[16,512]{1,0:T(8,128)S(1)}, f32[16,512]{1,0:T(8,128)S(1)}, u32[]{:S(2)}, u32[]{:S(2)}) collective-permute-start(f32[16,512]{1,0:T(8,128)S(1)} %get-tuple-element.875), channel_id=1, source_target_pairs={{0,1},{1,2},{2,3},{3,4},{4,5},{5,6},{6,7},{7,8},{8,9},{9,10},{10,1... | collective-permute-start | bytes 98312 | tf_op jit(solution)/shard_map/while/body/eval_jaxpr/ppermute | solution.py:10
  108.0 5.1 %collective-permute-start = (f32[16,512]{1,0:T(8,128)S(1)}, f32[16,512]{1,0:T(8,128)S(1)}, u32[]{:S(2)}, u32[]{:S(2)}) collective-permute-start(f32[16,512]{1,0:T(8,128)S(1)} %get-tuple-element.875), channel_id=1, source_target_pairs={{0,1},{1,2},{2,3},{3,4},{4,5},{5,6},{6,7},{7,8},{8,9},{9,10},{10,1... | collective-permute-start | bytes 98312 | tf_op jit(solution)/shard_map/while/body/eval_jaxpr/ppermute | solution.py:10
  114.1 5.1 %collective-permute-start = (f32[16,512]{1,0:T(8,128)S(1)}, f32[16,512]{1,0:T(8,128)S(1)}, u32[]{:S(2)}, u32[]{:S(2)}) collective-permute-start(f32[16,512]{1,0:T(8,128)S(1)} %get-tuple-element.875), channel_id=1, source_target_pairs={{0,1},{1,2},{2,3},{3,4},{4,5},{5,6},{6,7},{7,8},{8,9},{9,10},{10,1... | collective-permute-start | bytes 98312 | tf_op jit(solution)/shard_map/while/body/eval_jaxpr/ppermute | solution.py:10
  120.2 5.1 %collective-permute-start = (f32[16,512]{1,0:T(8,128)S(1)}, f32[16,512]{1,0:T(8,128)S(1)}, u32[]{:S(2)}, u32[]{:S(2)}) collective-permute-start(f32[16,512]{1,0:T(8,128)S(1)} %get-tuple-element.875), channel_id=1, source_target_pairs={{0,1},{1,2},{2,3},{3,4},{4,5},{5,6},{6,7},{7,8},{8,9},{9,10},{10,1... | collective-permute-start | bytes 98312 | tf_op jit(solution)/shard_map/while/body/eval_jaxpr/ppermute | solution.py:10
  126.4 5.1 %collective-permute-start = (f32[16,512]{1,0:T(8,128)S(1)}, f32[16,512]{1,0:T(8,128)S(1)}, u32[]{:S(2)}, u32[]{:S(2)}) collective-permute-start(f32[16,512]{1,0:T(8,128)S(1)} %get-tuple-element.875), channel_id=1, source_target_pairs={{0,1},{1,2},{2,3},{3,4},{4,5},{5,6},{6,7},{7,8},{8,9},{9,10},{10,1... | collective-permute-start | bytes 98312 | tf_op jit(solution)/shard_map/while/body/eval_jaxpr/ppermute | solution.py:10
  132.5 5.1 %collective-permute-start = (f32[16,512]{1,0:T(8,128)S(1)}, f32[16,512]{1,0:T(8,128)S(1)}, u32[]{:S(2)}, u32[]{:S(2)}) collective-permute-start(f32[16,512]{1,0:T(8,128)S(1)} %get-tuple-element.875), channel_id=1, source_target_pairs={{0,1},{1,2},{2,3},{3,4},{4,5},{5,6},{6,7},{7,8},{8,9},{9,10},{10,1... | collective-permute-start | bytes 98312 | tf_op jit(solution)/shard_map/while/body/eval_jaxpr/ppermute | solution.py:10
  138.6 5.1 %collective-permute-start = (f32[16,512]{1,0:T(8,128)S(1)}, f32[16,512]{1,0:T(8,128)S(1)}, u32[]{:S(2)}, u32[]{:S(2)}) collective-permute-start(f32[16,512]{1,0:T(8,128)S(1)} %get-tuple-element.875), channel_id=1, source_target_pairs={{0,1},{1,2},{2,3},{3,4},{4,5},{5,6},{6,7},{7,8},{8,9},{9,10},{10,1... | collective-permute-start | bytes 98312 | tf_op jit(solution)/shard_map/while/body/eval_jaxpr/ppermute | solution.py:10
  144.7 5.1 %collective-permute-start = (f32[16,512]{1,0:T(8,128)S(1)}, f32[16,512]{1,0:T(8,128)S(1)}, u32[]{:S(2)}, u32[]{:S(2)}) collective-permute-start(f32[16,512]{1,0:T(8,128)S(1)} %get-tuple-element.875), channel_id=1, source_target_pairs={{0,1},{1,2},{2,3},{3,4},{4,5},{5,6},{6,7},{7,8},{8,9},{9,10},{10,1... | collective-permute-start | bytes 98312 | tf_op jit(solution)/shard_map/while/body/eval_jaxpr/ppermute | solution.py:10
  150.9 5.1 %collective-permute-start = (f32[16,512]{1,0:T(8,128)S(1)}, f32[16,512]{1,0:T(8,128)S(1)}, u32[]{:S(2)}, u32[]{:S(2)}) collective-permute-start(f32[16,512]{1,0:T(8,128)S(1)} %get-tuple-element.875), channel_id=1, source_target_pairs={{0,1},{1,2},{2,3},{3,4},{4,5},{5,6},{6,7},{7,8},{8,9},{9,10},{10,1... | collective-permute-start | bytes 98312 | tf_op jit(solution)/shard_map/while/body/eval_jaxpr/ppermute | solution.py:10
  157.0 10.0 %while.88 = (s32[]{:T(128)}, f32[16,512]{1,0:T(8,128)S(1)}, f32[16,16,512]{2,1,0:T(8,128)S(1)}, f32[512,512]{1,0:T(8,128)S(1)}, s32[]{:T(128)}) while((s32[]{:T(128)}, f32[16,512]{1,0:T(8,128)S(1)}, f32[16,16,512]{2,1,0:T(8,128)S(1)}, f32[512,512]{1,0:T(8,128)S(1)}, s32[]{:T(128)}) %tuple.183), condition=%wide.region_7.8_spmd, body=%wide.region_6.7_spmd.sunk | while | flops 50331648 | bytes 1212481 | solution.py:63
  169.5 44.2 %while.89 = (s32[]{:T(128)}, f32[16,512]{1,0:T(8,128)S(1)}, f32[16,16,512]{2,1,0:T(8,128)S(1)}, f32[16,16,512]{2,1,0:T(8,128)}, f32[512,512]{1,0:T(8,128)S(1)}, ...) while((s32[]{:T(128)}, f32[16,512]{1,0:T(8,128)S(1)}, f32[16,16,512]{2,1,0:T(8,128)S(1)}, ...), condition=%wide.region_9.10_spmd, body=%wide.region_8.9_spmd.sunk | while | flops 100679680 | bytes 2326633 | solution.py:72
  221.1 93.1 %while.90 = (s32[]{:T(128)}, f32[16,512]{1,0:T(8,128)S(1)}, f32[16,512]{1,0:T(8,128)S(1)}, s32[]{:T(128)}, f32[512,512]{1,0:T(8,128)S(1)}, /*index=5*/f32[16,512]{1,0:T(8,128)S(1)}, s32[]{:T(128)}, s32[]{:T(128)}) while((s32[]{:T(128)}, f32[16,512]{1,0:T(8,128)S(1)}, f32[16,512]{1,0:T(8,128)S(1)}, s32[]{:T(128)}, ...), condition=%wide.region_13.14_spmd, body=%wide.region_10.13_spmd.sunk | while | flops 50339844 | bytes 1343703 | solution.py:83
  223.0 4.8 %collective-permute-done.1 = f32[16,512]{1,0:T(8,128)S(1)} collective-permute-done((f32[16,512]{1,0:T(8,128)S(1)}, f32[16,512]{1,0:T(8,128)S(1)}, u32[]{:S(2)}, u32[]{:S(2)}) %collective-permute-start.1) | collective-permute-done | bytes 32800 | tf_op jit(solution)/shard_map/while/body/eval_jaxpr/ppermute | solution.py:10
  248.1 4.2 %collective-permute-done.1 = f32[16,512]{1,0:T(8,128)S(1)} collective-permute-done((f32[16,512]{1,0:T(8,128)S(1)}, f32[16,512]{1,0:T(8,128)S(1)}, u32[]{:S(2)}, u32[]{:S(2)}) %collective-permute-start.1) | collective-permute-done | bytes 32800 | tf_op jit(solution)/shard_map/while/body/eval_jaxpr/ppermute | solution.py:10
  272.6 4.2 %collective-permute-done.1 = f32[16,512]{1,0:T(8,128)S(1)} collective-permute-done((f32[16,512]{1,0:T(8,128)S(1)}, f32[16,512]{1,0:T(8,128)S(1)}, u32[]{:S(2)}, u32[]{:S(2)}) %collective-permute-start.1) | collective-permute-done | bytes 32800 | tf_op jit(solution)/shard_map/while/body/eval_jaxpr/ppermute | solution.py:10
  297.7 4.2 %collective-permute-done.1 = f32[16,512]{1,0:T(8,128)S(1)} collective-permute-done((f32[16,512]{1,0:T(8,128)S(1)}, f32[16,512]{1,0:T(8,128)S(1)}, u32[]{:S(2)}, u32[]{:S(2)}) %collective-permute-start.1) | collective-permute-done | bytes 32800 | tf_op jit(solution)/shard_map/while/body/eval_jaxpr/ppermute | solution.py:10
  314.2 10.0 %while.91 = (s32[]{:T(128)}, f32[16,512]{1,0:T(8,128)S(1)}, f32[16,16,512]{2,1,0:T(8,128)S(1)}, f32[512,512]{1,0:T(8,128)S(1)}, s32[]{:T(128)}, /*index=5*/s32[]{:T(128)}) while((s32[]{:T(128)}, f32[16,512]{1,0:T(8,128)S(1)}, f32[16,16,512]{2,1,0:T(8,128)S(1)}, f32[512,512]{1,0:T(8,128)S(1)}, s32[]{:T(128)}, /*index=5*/s32[]{:T(128)}) %tuple.201), condition=%wide.region_15.16_spmd, body=%wide.region_14.15_spmd.sunk | while | flops 50331648 | bytes 1212501 | solution.py:89
  (286 shorter events, 234.9 us)
Async XLA Ops:
  70.6 6.1 %collective-permute-start = (f32[16,512]{1,0:T(8,128)S(1)}, f32[16,512]{1,0:T(8,128)S(1)}, u32[]{:S(2)}, u32[]{:S(2)}) collective-permute-start(f32[16,512]{1,0:T(8,128)S(1)} %get-tuple-element.875), channel_id=1, source_target_pairs={{0,1},{1,2},{2,3},{3,4},{4,5},{5,6},{6,7},{7,8},{8,9},{9,10},{10,1... | collective-permute-start | bytes 98312 | tf_op jit(solution)/shard_map/while/body/eval_jaxpr/ppermute | solution.py:10
  76.7 6.1 %collective-permute-start = (f32[16,512]{1,0:T(8,128)S(1)}, f32[16,512]{1,0:T(8,128)S(1)}, u32[]{:S(2)}, u32[]{:S(2)}) collective-permute-start(f32[16,512]{1,0:T(8,128)S(1)} %get-tuple-element.875), channel_id=1, source_target_pairs={{0,1},{1,2},{2,3},{3,4},{4,5},{5,6},{6,7},{7,8},{8,9},{9,10},{10,1... | collective-permute-start | bytes 98312 | tf_op jit(solution)/shard_map/while/body/eval_jaxpr/ppermute | solution.py:10
  89.0 6.8 %collective-permute-start = (f32[16,512]{1,0:T(8,128)S(1)}, f32[16,512]{1,0:T(8,128)S(1)}, u32[]{:S(2)}, u32[]{:S(2)}) collective-permute-start(f32[16,512]{1,0:T(8,128)S(1)} %get-tuple-element.875), channel_id=1, source_target_pairs={{0,1},{1,2},{2,3},{3,4},{4,5},{5,6},{6,7},{7,8},{8,9},{9,10},{10,1... | collective-permute-start | bytes 98312 | tf_op jit(solution)/shard_map/while/body/eval_jaxpr/ppermute | solution.py:10
  95.8 6.1 %collective-permute-start = (f32[16,512]{1,0:T(8,128)S(1)}, f32[16,512]{1,0:T(8,128)S(1)}, u32[]{:S(2)}, u32[]{:S(2)}) collective-permute-start(f32[16,512]{1,0:T(8,128)S(1)} %get-tuple-element.875), channel_id=1, source_target_pairs={{0,1},{1,2},{2,3},{3,4},{4,5},{5,6},{6,7},{7,8},{8,9},{9,10},{10,1... | collective-permute-start | bytes 98312 | tf_op jit(solution)/shard_map/while/body/eval_jaxpr/ppermute | solution.py:10
  101.9 6.1 %collective-permute-start = (f32[16,512]{1,0:T(8,128)S(1)}, f32[16,512]{1,0:T(8,128)S(1)}, u32[]{:S(2)}, u32[]{:S(2)}) collective-permute-start(f32[16,512]{1,0:T(8,128)S(1)} %get-tuple-element.875), channel_id=1, source_target_pairs={{0,1},{1,2},{2,3},{3,4},{4,5},{5,6},{6,7},{7,8},{8,9},{9,10},{10,1... | collective-permute-start | bytes 98312 | tf_op jit(solution)/shard_map/while/body/eval_jaxpr/ppermute | solution.py:10
  108.0 6.1 %collective-permute-start = (f32[16,512]{1,0:T(8,128)S(1)}, f32[16,512]{1,0:T(8,128)S(1)}, u32[]{:S(2)}, u32[]{:S(2)}) collective-permute-start(f32[16,512]{1,0:T(8,128)S(1)} %get-tuple-element.875), channel_id=1, source_target_pairs={{0,1},{1,2},{2,3},{3,4},{4,5},{5,6},{6,7},{7,8},{8,9},{9,10},{10,1... | collective-permute-start | bytes 98312 | tf_op jit(solution)/shard_map/while/body/eval_jaxpr/ppermute | solution.py:10
  114.1 6.1 %collective-permute-start = (f32[16,512]{1,0:T(8,128)S(1)}, f32[16,512]{1,0:T(8,128)S(1)}, u32[]{:S(2)}, u32[]{:S(2)}) collective-permute-start(f32[16,512]{1,0:T(8,128)S(1)} %get-tuple-element.875), channel_id=1, source_target_pairs={{0,1},{1,2},{2,3},{3,4},{4,5},{5,6},{6,7},{7,8},{8,9},{9,10},{10,1... | collective-permute-start | bytes 98312 | tf_op jit(solution)/shard_map/while/body/eval_jaxpr/ppermute | solution.py:10
  120.2 6.1 %collective-permute-start = (f32[16,512]{1,0:T(8,128)S(1)}, f32[16,512]{1,0:T(8,128)S(1)}, u32[]{:S(2)}, u32[]{:S(2)}) collective-permute-start(f32[16,512]{1,0:T(8,128)S(1)} %get-tuple-element.875), channel_id=1, source_target_pairs={{0,1},{1,2},{2,3},{3,4},{4,5},{5,6},{6,7},{7,8},{8,9},{9,10},{10,1... | collective-permute-start | bytes 98312 | tf_op jit(solution)/shard_map/while/body/eval_jaxpr/ppermute | solution.py:10
  126.4 6.1 %collective-permute-start = (f32[16,512]{1,0:T(8,128)S(1)}, f32[16,512]{1,0:T(8,128)S(1)}, u32[]{:S(2)}, u32[]{:S(2)}) collective-permute-start(f32[16,512]{1,0:T(8,128)S(1)} %get-tuple-element.875), channel_id=1, source_target_pairs={{0,1},{1,2},{2,3},{3,4},{4,5},{5,6},{6,7},{7,8},{8,9},{9,10},{10,1... | collective-permute-start | bytes 98312 | tf_op jit(solution)/shard_map/while/body/eval_jaxpr/ppermute | solution.py:10
  132.5 6.1 %collective-permute-start = (f32[16,512]{1,0:T(8,128)S(1)}, f32[16,512]{1,0:T(8,128)S(1)}, u32[]{:S(2)}, u32[]{:S(2)}) collective-permute-start(f32[16,512]{1,0:T(8,128)S(1)} %get-tuple-element.875), channel_id=1, source_target_pairs={{0,1},{1,2},{2,3},{3,4},{4,5},{5,6},{6,7},{7,8},{8,9},{9,10},{10,1... | collective-permute-start | bytes 98312 | tf_op jit(solution)/shard_map/while/body/eval_jaxpr/ppermute | solution.py:10
  138.6 6.1 %collective-permute-start = (f32[16,512]{1,0:T(8,128)S(1)}, f32[16,512]{1,0:T(8,128)S(1)}, u32[]{:S(2)}, u32[]{:S(2)}) collective-permute-start(f32[16,512]{1,0:T(8,128)S(1)} %get-tuple-element.875), channel_id=1, source_target_pairs={{0,1},{1,2},{2,3},{3,4},{4,5},{5,6},{6,7},{7,8},{8,9},{9,10},{10,1... | collective-permute-start | bytes 98312 | tf_op jit(solution)/shard_map/while/body/eval_jaxpr/ppermute | solution.py:10
  144.7 6.1 %collective-permute-start = (f32[16,512]{1,0:T(8,128)S(1)}, f32[16,512]{1,0:T(8,128)S(1)}, u32[]{:S(2)}, u32[]{:S(2)}) collective-permute-start(f32[16,512]{1,0:T(8,128)S(1)} %get-tuple-element.875), channel_id=1, source_target_pairs={{0,1},{1,2},{2,3},{3,4},{4,5},{5,6},{6,7},{7,8},{8,9},{9,10},{10,1... | collective-permute-start | bytes 98312 | tf_op jit(solution)/shard_map/while/body/eval_jaxpr/ppermute | solution.py:10
  150.9 6.1 %collective-permute-start = (f32[16,512]{1,0:T(8,128)S(1)}, f32[16,512]{1,0:T(8,128)S(1)}, u32[]{:S(2)}, u32[]{:S(2)}) collective-permute-start(f32[16,512]{1,0:T(8,128)S(1)} %get-tuple-element.875), channel_id=1, source_target_pairs={{0,1},{1,2},{2,3},{3,4},{4,5},{5,6},{6,7},{7,8},{8,9},{9,10},{10,1... | collective-permute-start | bytes 98312 | tf_op jit(solution)/shard_map/while/body/eval_jaxpr/ppermute | solution.py:10
  221.1 6.7 %collective-permute-start.1 = (f32[16,512]{1,0:T(8,128)S(1)}, f32[16,512]{1,0:T(8,128)S(1)}, u32[]{:S(2)}, u32[]{:S(2)}) collective-permute-start(f32[16,512]{1,0:T(8,128)S(1)} %get-tuple-element.936), channel_id=1, source_target_pairs={{1,0},{2,1},{3,2},{4,3},{5,4},{6,5},{7,6},{8,7},{9,8},{10,9},{11,1... | collective-permute-start | bytes 98312 | tf_op jit(solution)/shard_map/while/body/eval_jaxpr/ppermute | solution.py:10
  227.8 6.1 %collective-permute-start.1 = (f32[16,512]{1,0:T(8,128)S(1)}, f32[16,512]{1,0:T(8,128)S(1)}, u32[]{:S(2)}, u32[]{:S(2)}) collective-permute-start(f32[16,512]{1,0:T(8,128)S(1)} %get-tuple-element.936), channel_id=1, source_target_pairs={{1,0},{2,1},{3,2},{4,3},{5,4},{6,5},{7,6},{8,7},{9,8},{10,9},{11,1... | collective-permute-start | bytes 98312 | tf_op jit(solution)/shard_map/while/body/eval_jaxpr/ppermute | solution.py:10
  233.9 6.1 %collective-permute-start.1 = (f32[16,512]{1,0:T(8,128)S(1)}, f32[16,512]{1,0:T(8,128)S(1)}, u32[]{:S(2)}, u32[]{:S(2)}) collective-permute-start(f32[16,512]{1,0:T(8,128)S(1)} %get-tuple-element.936), channel_id=1, source_target_pairs={{1,0},{2,1},{3,2},{4,3},{5,4},{6,5},{7,6},{8,7},{9,8},{10,9},{11,1... | collective-permute-start | bytes 98312 | tf_op jit(solution)/shard_map/while/body/eval_jaxpr/ppermute | solution.py:10
  240.0 6.1 %collective-permute-start.1 = (f32[16,512]{1,0:T(8,128)S(1)}, f32[16,512]{1,0:T(8,128)S(1)}, u32[]{:S(2)}, u32[]{:S(2)}) collective-permute-start(f32[16,512]{1,0:T(8,128)S(1)} %get-tuple-element.936), channel_id=1, source_target_pairs={{1,0},{2,1},{3,2},{4,3},{5,4},{6,5},{7,6},{8,7},{9,8},{10,9},{11,1... | collective-permute-start | bytes 98312 | tf_op jit(solution)/shard_map/while/body/eval_jaxpr/ppermute | solution.py:10
  246.2 6.1 %collective-permute-start.1 = (f32[16,512]{1,0:T(8,128)S(1)}, f32[16,512]{1,0:T(8,128)S(1)}, u32[]{:S(2)}, u32[]{:S(2)}) collective-permute-start(f32[16,512]{1,0:T(8,128)S(1)} %get-tuple-element.936), channel_id=1, source_target_pairs={{1,0},{2,1},{3,2},{4,3},{5,4},{6,5},{7,6},{8,7},{9,8},{10,9},{11,1... | collective-permute-start | bytes 98312 | tf_op jit(solution)/shard_map/while/body/eval_jaxpr/ppermute | solution.py:10
  252.3 6.1 %collective-permute-start.1 = (f32[16,512]{1,0:T(8,128)S(1)}, f32[16,512]{1,0:T(8,128)S(1)}, u32[]{:S(2)}, u32[]{:S(2)}) collective-permute-start(f32[16,512]{1,0:T(8,128)S(1)} %get-tuple-element.936), channel_id=1, source_target_pairs={{1,0},{2,1},{3,2},{4,3},{5,4},{6,5},{7,6},{8,7},{9,8},{10,9},{11,1... | collective-permute-start | bytes 98312 | tf_op jit(solution)/shard_map/while/body/eval_jaxpr/ppermute | solution.py:10
  258.4 6.1 %collective-permute-start.1 = (f32[16,512]{1,0:T(8,128)S(1)}, f32[16,512]{1,0:T(8,128)S(1)}, u32[]{:S(2)}, u32[]{:S(2)}) collective-permute-start(f32[16,512]{1,0:T(8,128)S(1)} %get-tuple-element.936), channel_id=1, source_target_pairs={{1,0},{2,1},{3,2},{4,3},{5,4},{6,5},{7,6},{8,7},{9,8},{10,9},{11,1... | collective-permute-start | bytes 98312 | tf_op jit(solution)/shard_map/while/body/eval_jaxpr/ppermute | solution.py:10
  264.5 6.1 %collective-permute-start.1 = (f32[16,512]{1,0:T(8,128)S(1)}, f32[16,512]{1,0:T(8,128)S(1)}, u32[]{:S(2)}, u32[]{:S(2)}) collective-permute-start(f32[16,512]{1,0:T(8,128)S(1)} %get-tuple-element.936), channel_id=1, source_target_pairs={{1,0},{2,1},{3,2},{4,3},{5,4},{6,5},{7,6},{8,7},{9,8},{10,9},{11,1... | collective-permute-start | bytes 98312 | tf_op jit(solution)/shard_map/while/body/eval_jaxpr/ppermute | solution.py:10
  270.7 6.1 %collective-permute-start.1 = (f32[16,512]{1,0:T(8,128)S(1)}, f32[16,512]{1,0:T(8,128)S(1)}, u32[]{:S(2)}, u32[]{:S(2)}) collective-permute-start(f32[16,512]{1,0:T(8,128)S(1)} %get-tuple-element.936), channel_id=1, source_target_pairs={{1,0},{2,1},{3,2},{4,3},{5,4},{6,5},{7,6},{8,7},{9,8},{10,9},{11,1... | collective-permute-start | bytes 98312 | tf_op jit(solution)/shard_map/while/body/eval_jaxpr/ppermute | solution.py:10
  295.8 6.1 %collective-permute-start.1 = (f32[16,512]{1,0:T(8,128)S(1)}, f32[16,512]{1,0:T(8,128)S(1)}, u32[]{:S(2)}, u32[]{:S(2)}) collective-permute-start(f32[16,512]{1,0:T(8,128)S(1)} %get-tuple-element.936), channel_id=1, source_target_pairs={{1,0},{2,1},{3,2},{4,3},{5,4},{6,5},{7,6},{8,7},{9,8},{10,9},{11,1... | collective-permute-start | bytes 98312 | tf_op jit(solution)/shard_map/while/body/eval_jaxpr/ppermute | solution.py:10
  301.9 6.1 %collective-permute-start.1 = (f32[16,512]{1,0:T(8,128)S(1)}, f32[16,512]{1,0:T(8,128)S(1)}, u32[]{:S(2)}, u32[]{:S(2)}) collective-permute-start(f32[16,512]{1,0:T(8,128)S(1)} %get-tuple-element.936), channel_id=1, source_target_pairs={{1,0},{2,1},{3,2},{4,3},{5,4},{6,5},{7,6},{8,7},{9,8},{10,9},{11,1... | collective-permute-start | bytes 98312 | tf_op jit(solution)/shard_map/while/body/eval_jaxpr/ppermute | solution.py:10
  (28 other events, 72.4 us)
where the time goes:
time: 329 us; the launch traced here: 325 us
  matrix products  137 us (42%)
  starting transfers between devices  104 us (32%)
  waiting for transfers between devices  78.5 us (24%)
    dot_general x125, matrix products, product(): jnp.dot(first_op, second_op, precision=lax.Precision.HIGHEST, preferred_e...  137 us
    ppermute x30, starting transfers between devices, passed_along(): return lax.ppermute(x, axis, pairs)  104 us
    ppermute x30, waiting for transfers between devices, passed_along(): return lax.ppermute(x, axis, pairs)  78.5 us
  transfers between devices with their start and end apart: 30, of which 30 were waited for; matrix products, arithmetic and copies ran while one was open for 0% of the time, Pallas kernels for 0%

commit v1 on v0

v1 whole, which is shorter than its diff:
```python
import functools

import jax
import jax.numpy as jnp
from jax import lax
from jax.experimental import pallas as pl
from jax.experimental.pallas import tpu as pltpu
from jax.sharding import PartitionSpec as P

MESH = pl.DeviceIdType.MESH


def log2(n):
    return n.bit_length() - 1


def radices_of(bits):
    return [2] * (bits // 2) + [1] * (bits % 2)


def messages_of(devices):
    rounds = radices_of(log2(devices))
    out, stride = [], 1
    for r, bits in enumerate(rounds):
        last = r == len(rounds) - 1
        for term in range(2**bits):
            distance = term * stride + (1 if last else 0)
            if 0 < distance < devices:
                out.append((r, term, distance))
        stride *= 2**bits
    return out


def mm(a, b):
    return jnp.dot(a, b, preferred_element_type=jnp.float32)


def split(x):
    high = x.astype(jnp.bfloat16)
    return high, (x - high.astype(jnp.float32)).astype(jnp.bfloat16)


def product(a, w):
    high, low = split(a)
    rows = a.shape[0]
    both = mm(jnp.concatenate([high, low], axis=0), w[0])
    return both[:rows] + both[rows:] + mm(high, w[1])


def apply(a, w):
    return a + product(a, w)


def less_identity(m):
    row = lax.broadcasted_iota(jnp.int32, m.shape, 0)
    column = lax.broadcasted_iota(jnp.int32, m.shape, 1)
    return m - jnp.where(row == column, 1.0, 0.0)


def keep(w, x):
    w[0], w[1] = split(x)


def square(dst, src, tile=256):
    def body(i, c):
        rows = pl.ds(pl.multiple_of(i * tile, tile), tile)
        high, low = src[0, rows, :], src[1, rows, :]
        x = mm(high, src[0]) + mm(low, src[0]) + mm(high, src[1])
        e = high.astype(jnp.float32) + low.astype(jnp.float32)
        dst[0, rows, :], dst[1, rows, :] = split(x + 2.0 * e)
        return c

    lax.fori_loop(0, src.shape[1] // tile, body, 0)


def kernel(devices, steps, y_ref, start_ref, a_ref, h_ref, k_ref, g_ref, f_out, s_out,
           aw, hw, kw, fpow, gpow, x, z, ends, inbox, send_sem, recv_sem):
    me = lax.axis_index("tm")
    b = start_ref.shape[0]
    local_bits, hop_bits = log2(steps), log2(devices)
    rounds = radices_of(hop_bits)
    messages = messages_of(devices)
    distances = sorted({m[2] for m in messages})

    barrier = pltpu.get_barrier_semaphore()
    for d in distances:
        for sign in (1, -1):
            other = me + sign * d

            @pl.when((other >= 0) & (other < devices))
            def _():
                pl.semaphore_signal(barrier, inc=1, device_id={"tm": other}, device_id_type=MESH)

    keep(aw, less_identity(a_ref[...]))
    keep(hw, h_ref[...])
    keep(kw, k_ref[...])
    keep(gpow.at[0], less_identity(g_ref[...]))
    x[...] = product(y_ref[...], kw)
    h = h_ref[...] + product(less_identity(a_ref[...]), hw)
    keep(fpow.at[0], less_identity(a_ref[...]) - product(h, kw))

    @pl.when(me == 0)
    def _():
        x[:b, :] += apply(start_ref[...], fpow.at[0])

    for j in range(local_bits):
        shift = b << j
        x[shift:, :] += apply(x[:-shift, :], fpow.at[j])
        square(fpow.at[j + 1], fpow.at[j])

    peers = 0
    for d in distances:
        peers += jnp.where(me >= d, 1, 0) + jnp.where(me + d < devices, 1, 0)
    pl.semaphore_wait(barrier, peers)

    def copy(way, r, index, distance):
        return pltpu.make_async_remote_copy(
            src_ref=ends.at[way, r],
            dst_ref=inbox.at[way, index],
            send_sem=send_sem.at[way, index],
            recv_sem=recv_sem.at[way, index],
            device_id={"tm": me + distance * (1 - 2 * way)},
            device_id_type=MESH,
        )

    def exchange(way, value, powers, beside):
        sends = lambda d: (me + d < devices) if way == 0 else (me >= d)
        gets = lambda d: (me >= d) if way == 0 else (me + d < devices)
        level = 0
        for r, bits in enumerate(rounds):
            ends[way, r] = value
            mine = [(i, m[1], m[2]) for i, m in enumerate(messages) if m[0] == r]
            for i, term, d in mine:
                @pl.when(sends(d))
                def _():
                    copy(way, r, i, d).start()

                @pl.when(jnp.logical_not(gets(d)))
                def _():
                    inbox[way, i] = jnp.zeros(inbox.shape[2:], jnp.float32)
            beside(r)
            for i, term, d in mine:
                @pl.when(gets(d))
                def _():
                    copy(way, r, i, d).wait_recv()
            terms = {0: value}
            for i, term, d in mine:
                terms[term] = inbox[way, i]
            terms = [terms.get(t, jnp.zeros_like(value)) for t in range(2**bits)]
            for k in range(bits):
                odd = jnp.concatenate(terms[1::2], axis=0) if len(terms) > 2 else terms[1]
                moved = apply(odd, powers.at[level + k])
                terms = [terms[2 * i] + moved[i * b:(i + 1) * b] for i in range(len(terms) // 2)]
            value = terms[0]
            level += bits
        for i, m in enumerate(messages):
            @pl.when(sends(m[2]))
            def _():
                copy(way, m[0], i, m[2]).wait_send()
        return value

    def beside_forward(r):
        done = sum(rounds[:r])
        first = [local_bits + done + k for k in range(rounds[r] - (1 if r == 0 else 0))]
        for j in first:
            if j + 1 < local_bits + hop_bits and r == 0:
                square(fpow.at[j + 1], fpow.at[j])
        if r == 0:
            for j in range(local_bits):
                square(gpow.at[j + 1], gpow.at[j])
        if r > 0:
            for j in range(local_bits + done - 1, local_bits + done + rounds[r] - 1):
                square(fpow.at[j + 1], fpow.at[j])

    entering = exchange(0, x[-b:, :], fpow.at[pl.ds(local_bits, hop_bits)], beside_forward)

    z[:b, :] = apply(entering, fpow.at[0])
    for j in range(local_bits):
        n = b << j
        z[n:2 * n, :] = apply(z[:n, :], fpow.at[j])
    x[...] += z[...]
    f_out[...] = x[...]
    last = x[-b:, :]
    step = product(x[...], aw)
    x[...] = -step - product(x[...] + step, gpow.at[0])

    @pl.when(me == devices - 1)
    def _():
        x[-b:, :] = last

    for j in range(local_bits):
        shift = b << j
        x[:-shift, :] += apply(x[shift:, :], gpow.at[j])

    def beside_backward(r):
        done = sum(rounds[:r])
        for j in range(local_bits + max(done - 1, 0), local_bits + done + rounds[r] - 1):
            square(gpow.at[j + 1], gpow.at[j])

    leaving = exchange(1, x[:b, :], gpow.at[pl.ds(local_bits, hop_bits)], beside_backward)
    total = b * steps
    z[total - b:, :] = apply(leaving, gpow.at[0])
    for j in range(local_bits):
        n = b << j
        z[total - 2 * n:total - n, :] = apply(z[total - n:, :], gpow.at[j])
    s_out[...] = x[...] + z[...]


def per_device(devices, y, start, a, h, k, g):
    steps, b, ny = y.shape
    ns = a.shape[0]
    powers = log2(steps) + log2(devices)
    count = len(messages_of(devices))
    two = lambda *shape: pltpu.VMEM((2,) + shape, jnp.bfloat16)
    rows = steps * b
    f, s = pl.pallas_call(
        functools.partial(kernel, devices, steps),
        out_shape=[jax.ShapeDtypeStruct((rows, ns), jnp.float32)] * 2,
        in_specs=[pl.BlockSpec(memory_space=pltpu.VMEM)] * 6,
        out_specs=[pl.BlockSpec(memory_space=pltpu.VMEM)] * 2,
        scratch_shapes=[
            two(ns, ns), two(ns, ny), two(ny, ns),
            pltpu.VMEM((powers, 2, ns, ns), jnp.bfloat16),
            pltpu.VMEM((powers, 2, ns, ns), jnp.bfloat16),
            pltpu.VMEM((rows, ns), jnp.float32),
            pltpu.VMEM((rows, ns), jnp.float32),
            pltpu.VMEM((2, len(radices_of(log2(devices))), b, ns), jnp.float32),
            pltpu.VMEM((2, count, b, ns), jnp.float32),
            pltpu.SemaphoreType.DMA((2, count)),
            pltpu.SemaphoreType.DMA((2, count)),
        ],
        compiler_params=pltpu.CompilerParams(
            collective_id=0, has_side_effects=True, vmem_limit_bytes=56 * 1024 * 1024
        ),
    )(y.reshape(rows, ny), start, a, h, k, g)
    return f.reshape(steps, b, ns), s.reshape(steps, b, ns)


def solution(mesh):
    in_specs = (P(("groups", "tm"), None, None), P("groups", None), P(), P(), P(), P())
    out_specs = (P(("groups", "tm"), None, None), P(("groups", "tm"), None, None))
    return jax.shard_map(
        functools.partial(per_device, mesh.shape["tm"]),
        mesh=mesh, in_specs=in_specs, out_specs=out_specs, check_vma=False,
    )
```

time: 329 us -> 44.7 us (0.14)
  the two profiles are of different devices: /device:TPU:7 before, /device:TPU:0 now
where the time goes in v1:
time: 44.7 us; the launch traced here: 44.6 us
  Pallas kernels  41.2 us (92%)
  local copies, waits for them, and re-layouts  2.74 us (6%)
  between operations  0.65 us (1%)
    pallas_call x1, Pallas kernels, per_device(): pl.pallas_call(functools.partial(kernel, devices, steps), out_shape=[jax....  41.2 us
    unnamed x4, local copies, waits for them, and re-layouts  2.74 us

profile of v1, /device:TPU:0, one launch (start us, length us, event | category | flops | bytes accessed | tf_op | source)
XLA Modules:
  0.0 44.6 jit_solution(16003780928343069898)
XLA Ops:
  0.6 41.2 %shard_map.77 = (f32[256,512]{1,0:T(8,128)}, f32[256,512]{1,0:T(8,128)}) custom-call(f32[256,256]{1,0:T(8,128)} %bitcast.5, f32[16,512]{1,0:T(8,128)} %start_ref.1, f32[512,512]{1,0:T(8,128)} %a_ref.1, f32[512,256]{1,0:T(8,128)} %h_ref.1, f32[256,512]{1,0:T(8,128)} %k_ref.1, f32[512,512]{1,0:T(8,128)} %g_ref.1), custom_call_target="tpu_custom_call" | custom-call | tf_op jit(solution)/shard_map/pallas_call | solution.py:216
  41.8 0.0 copy-start
  41.8 1.9 %copy.10 = f32[16,16,512]{2,1,0:T(8,128)} copy(f32[16,16,512]{2,1,0:T(8,128)} %bitcast.4) | data formatting | bytes 1048576
  43.8 0.0 copy-done
  43.8 0.8 %copy.11 = f32[16,16,512]{2,1,0:T(8,128)} copy(f32[16,16,512]{2,1,0:T(8,128)S(1)} %bitcast.3) | data formatting | bytes 1048576
Async XLA Ops:
  41.8 2.0 %copy-start = (f32[256,512]{1,0:T(8,128)S(1)}, f32[256,512]{1,0:T(8,128)}, u32[]{:S(2)}) copy-start(f32[256,512]{1,0:T(8,128)} %get-tuple-element.5) | copy-start | bytes 1572868
